TPU v7x, 32 devices: a whole 2x2x4 slice. The times are simulated.
32 devices in a mesh: row: 16 (over z, y, core), col: 2 (over x).
Axes of the slice: x: 2, y: 2, z: 4, core: 2. Of those that a mesh axis runs over, the one named last changes fastest.
Arguments:
- integrals: bfloat16 [32768, 32768], P('row', 'col'), may hold values from -0.03125 to 0.03125
- amplitudes: bfloat16 [32768, 1024], P(('col', 'row')), may hold values from -6 to 6
- source: float32 [32768, 1024], P(('row', 'col')), may hold values from -6 to 6
- occ_energy: float32 [64], replicated, may hold values from -2.5 to -0.5
- vir_energy: float32 [512], replicated, may hold values from 0.3 to 3
- col_energy: float32 [1024], replicated, may hold values from 0.8 to 3
Outputs:
- new_amplitudes: float32 [32768, 1024], P(('row', 'col'))
All inputs are finite; a program needn't handle non-finite values.
Results may differ from a plain program's by a relative error of at most 0.0003.
Values may be sent and summed in bfloat16 or wider, within the bound.
A program may use at most 320 MiB of HBM per device.

v0:
```python
import jax
import jax.numpy as jnp
from jax import lax
from jax.sharding import PartitionSpec as P

VIRT = 512


def summed_terms(integrals, gathered):
    local_rows = integrals.shape[0]
    occ_rows = local_rows // VIRT
    occ_cols = integrals.shape[1] // VIRT
    columns = gathered.shape[1]
    blocks = integrals.reshape(occ_rows, VIRT, occ_cols, VIRT)
    amp_blocks = gathered.reshape(occ_cols, VIRT, columns)
    exchange_part = lax.dot_general(
        blocks, amp_blocks, (((1, 2), (1, 0)), ((), ())), preferred_element_type=jnp.float32
    )
    exchange_part = exchange_part.reshape(local_rows, columns)

    def both_rows(start, count):
        cycle_part = jnp.dot(integrals, gathered, preferred_element_type=jnp.float32)
        return cycle_part + exchange_part

    return both_rows


def half_sum(integrals, gathered, out_rows):
    both_rows = summed_terms(integrals, gathered)
    return lax.psum_scatter(
        both_rows(jnp.int32(0), lax.axis_size("col") * out_rows),
        "col",
        scatter_dimension=0,
        tiled=True,
    )


def per_device(integrals, amplitudes, source, occ_energy, vir_energy, col_energy):
    gathered = lax.all_gather(amplitudes, "row", axis=0, tiled=True)
    out_rows = source.shape[0]
    columns = gathered.shape[1]
    half = columns // 2
    pieces = []
    for which in range(2):
        pieces.append(half_sum(integrals, gathered[:, which * half : (which + 1) * half], out_rows))
    summed = jnp.concatenate(pieces, axis=1)
    first = (lax.axis_index("row") * lax.axis_size("col") + lax.axis_index("col")) * out_rows
    vir_all = jnp.tile(vir_energy, occ_energy.shape[0])
    occ_all = jnp.repeat(occ_energy, VIRT)
    vir_part = lax.dynamic_slice_in_dim(vir_all, first, out_rows, 0)
    occ_part = lax.dynamic_slice_in_dim(occ_all, first, out_rows, 0)
    denom = vir_part[:, None] - occ_part[:, None] + col_energy[None, :]
    return -(source + summed) / denom


def solution(mesh):
    in_specs = (P("row", "col"), P(("col", "row"), None), P(("row", "col"), None), P(), P(), P())
    out_specs = P(("row", "col"), None)
    return jax.shard_map(
        per_device, mesh=mesh, in_specs=in_specs, out_specs=out_specs, check_vma=False
    )
```

profile of v0, /device:TPU:0, one launch (start us, length us, event | category | flops | bytes accessed | tf_op | source)
XLA Modules:
  0.0 475.2 jit_solution(13319214924634415640)
XLA Ops:
  6.5 0.0 copy-start
  6.5 0.0 all-gather.2.cloned.1.call-start
  6.5 0.7 all-gather.2.cloned.1.call-update
  7.3 0.0 reduce-scatter.5.cloned.1.call-start
  7.3 44.7 %copy.8 = bf16[256,8,32,512]{3,2,1,0:T(8,128)(2,1)} copy(bf16[256,8,32,512]{3,1,2,0:T(8,128)(2,1)} %bitcast.6) | data formatting | bytes 134217728
  52.0 45.2 %bitcast_bitcast_fusion = bf16[4,512,512,32]{1,3,2,0:T(8,128)(2,1)} fusion(bf16[4,512,32,512]{3,2,1,0:T(8,128)(2,1)} %bitcast.25), kind=kLoop, calls=%fused_computation | loop fusion | bytes 134217728 | tf_op jit(solution)/shard_map/dot_general | solution.py:16
  97.1 102.0 %copy.7 = bf16[4,512,512,32]{2,1,0,3:T(8,128)(2,1)} copy(bf16[4,512,512,32]{1,3,2,0:T(8,128)(2,1)} %bitcast_bitcast_fusion) | data formatting | bytes 134217728 | tf_op jit(solution)/shard_map/dot_general | solution.py:16
  199.1 0.0 all-gather.2.cloned.1.call-done
  199.1 22.6 %fusion.4 = (bf16[16384,512]{1,0:T(8,128)(2,1)}, bf16[16384,512]{1,0:T(8,128)(2,1)}) fusion(bf16[16384,1024]{1,0:T(8,128)(2,1)} %all-gather.2.cloned.1.call-done), kind=kLoop, calls=%fused_computation.11 | loop fusion | bytes 67108864 | tf_op jit(solution)/shard_map/slice | solution.py:45
  221.7 44.6 %fusion.6 = f32[2048,512,1]{1,0,2:T(8,128)} fusion(bf16[2048,512,32]{1,0,2:T(8,128)(2,1)} %bitcast.1, bf16[32,512,512]{2,1,0:T(8,128)(2,1)} %bitcast.27), kind=kOutput, calls=%fused_computation.13 | convolution fusion | flops 34359738368 | bytes 88080384 | tf_op jit(solution)/shard_map/dot_general | solution.py:16
  266.3 46.3 %bitcast_add_fusion = f32[2048,512]{1,0:T(8,128)} fusion(f32[2048,512,1]{1,0,2:T(8,128)} %fusion.6, bf16[2048,16384]{1,0:T(8,128)(2,1)} %param.6, bf16[16384,1024]{1,0:T(8,128)(2,1)} %all-gather.2.cloned.1.call-done), kind=kOutput, calls=%fused_computation.4 | convolution fusion | flops 34360786944 | bytes 92274688 | tf_op jit(solution)/shard_map/dot_general | solution.py:22
  312.6 0.0 reduce-scatter.5.cloned.1.call-update
  312.6 0.0 reduce-scatter.3.cloned.1.call-start
  312.6 44.8 %fusion.5 = f32[2048,512,1]{1,0,2:T(8,128)} fusion(bf16[2048,512,32]{1,0,2:T(8,128)(2,1)} %bitcast.1, bf16[32,512,512]{2,1,0:T(8,128)(2,1)} %bitcast.26), kind=kOutput, calls=%fused_computation.12 | convolution fusion | flops 34359738368 | bytes 88080384 | tf_op jit(solution)/shard_map/dot_general | solution.py:16
  357.4 0.0 copy-start.2
  357.4 0.0 copy-start.1
  357.4 46.7 %bitcast_add_fusion.1 = f32[2048,512]{1,0:T(8,128)} fusion(f32[2048,512,1]{1,0,2:T(8,128)} %fusion.5, bf16[2048,16384]{1,0:T(8,128)(2,1)} %param.6, bf16[16384,1024]{1,0:T(8,128)(2,1)} %all-gather.2.cloned.1.call-done), kind=kOutput, calls=%fused_computation.5 | convolution fusion | flops 34360786944 | bytes 92274688 | tf_op jit(solution)/shard_map/dot_general | solution.py:22
  404.1 0.0 reduce-scatter.3.cloned.1.call-update
  404.1 0.0 copy-done.2
  404.1 0.1 broadcast_bitcast_fusion
  404.3 0.0 copy-done
  404.3 0.0 reduce-scatter.5.cloned.1.call-done
  404.4 58.0 %reduce-scatter.3.cloned.1.call-done = f32[1024,512]{1,0:T(8,128)} async-done(((f32[2048,512]{1,0:T(8,128)}), f32[1024,512]{1,0:T(8,128)}) %reduce-scatter.3.cloned.1.call-update) | async-done | bytes 2097168 | tf_op jit(solution)/shard_map/reduce_scatter | solution.py:30
  462.4 0.0 copy-done.1
  462.4 6.3 %fusion.1 = f32[1024,1024]{1,0:T(8,128)} fusion(f32[1024,1024]{1,0:T(8,128)} %param.8, f32[1024,512]{1,0:T(8,128)} %reduce-scatter.5.cloned.1.call-done, f32[1024,512]{1,0:T(8,128)} %reduce-scatter.3.cloned.1.call-done, f32[1024]{0:T(1024)S(1)} %copy-done.1, f32[1024]{0:T(1024)S(1)} %dynamic-slice_subtract_fusion), kind=kLoop, calls=%fused_computation.3 | loop fusion | flops 5242880 | bytes 12591104 | tf_op jit(solution)/shard_map/div | solution.py:53
  (4 shorter events, 0.1 us)
Async XLA Ops:
  6.5 397.7 %copy-start = (f32[512]{0:T(512)S(1)}, f32[512]{0:T(512)}, u32[]{:S(2)}) copy-start(f32[512]{0:T(512)} %param.10) | copy-start | bytes 6148
  6.5 192.6 %all-gather.2.cloned.1.call-start = ((), (), s32[]{:S(2)}) async-start(), calls=%async_computation.2 | async-start | bytes 35651584 | tf_op jit(solution)/shard_map/all_gather | solution.py:39
  7.3 397.1 %reduce-scatter.5.cloned.1.call-start = ((), (), s32[]{:S(2)}) async-start(), calls=%async_computation.4 | async-start | bytes 6291456 | tf_op jit(solution)/shard_map/reduce_scatter | solution.py:30
  312.6 149.8 %reduce-scatter.3.cloned.1.call-start = ((), (), s32[]{:S(2)}) async-start(), calls=%async_computation.3 | async-start | bytes 6291456 | tf_op jit(solution)/shard_map/reduce_scatter | solution.py:30
  357.4 46.7 %copy-start.2 = (f32[64]{0:T(128)S(1)}, f32[64]{0:T(128)}, u32[]{:S(2)}) copy-start(f32[64]{0:T(128)} %param.9) | copy-start | bytes 772
  357.4 105.0 %copy-start.1 = (f32[1024]{0:T(1024)S(1)}, f32[1024]{0:T(1024)}, u32[]{:S(2)}) copy-start(f32[1024]{0:T(1024)} %param.11) | copy-start | bytes 12292
Sparse Core Ops, SparseCore 0:
  9.0 170.7 all-gather.1
  312.7 58.1 reduce-scatter.4
  404.2 58.1 reduce-scatter.2
where the time goes:
time: 478 us; the launch traced here: 475 us
  local copies, waits for them, and re-layouts  215 us (45%)
  matrix products  182 us (38%)
  waiting for transfers between devices  58.8 us (12%)
  between operations  13.2 us (3%)
  other arithmetic  6.3 us (1%)
    dot_general x2, local copies, waits for them, and re-layouts, summed_terms(): lax.dot_general(blocks, amp_blocks, (((1, 2), (1, 0)), ((), ())), preferr...  147 us
    dot_general x2, matrix products, both_rows(): jnp.dot(integrals, gathered, preferred_element_type=jnp.float32)  93 us
    dot_general x2, matrix products, summed_terms(): lax.dot_general(blocks, amp_blocks, (((1, 2), (1, 0)), ((), ())), preferr...  89.3 us
    reduce_scatter x2, waiting for transfers between devices, half_sum(): lax.psum_scatter(both_rows(jnp.int32(0), lax.axis_size('col') * out_rows)...  58.1 us
    unnamed x11, local copies, waits for them, and re-layouts  44.8 us
    slice x1, local copies, waits for them, and re-layouts, per_device(): gathered[:, which * half:(which + 1) * half]  22.6 us
  transfers between devices with their start and end apart: 3, of which 1 were waited for; matrix products, arithmetic and copies ran while one was open for 60% of the time, Pallas kernels for 0%

commit v1 on v0

v1 whole, which is shorter than its diff:
```python
import functools

import jax
import jax.numpy as jnp
from jax import lax
from jax.experimental import pallas as pl
from jax.experimental.pallas import tpu as pltpu
from jax.sharding import PartitionSpec as P

VMEM_BYTES = 58 * 1024 * 1024
SMALL = jnp.float8_e5m2
REST_SCALE = 2.0**28
AMP_SCALE = 2.0**12
UNSCALE = 1.0 / (REST_SCALE * AMP_SCALE)


def pair_sum_kernel(block_ref, head_ref, rest_ref, *, virt):
    for at in range(block_ref.shape[1] // virt):
        columns = slice(at * virt, (at + 1) * virt)
        block = block_ref[:, columns]
        both = block.astype(jnp.float32) + block.T.astype(jnp.float32)
        head = both.astype(jnp.bfloat16)
        rest = (both - head.astype(jnp.float32)) * REST_SCALE
        head_ref[:, columns] = head
        rest_ref[:, columns] = rest.astype(SMALL)


def pair_sum(integrals, virt):
    rows, columns = integrals.shape
    wide = min(columns, 4 * virt)
    out_map = lambda i, j: (i, j)
    kernel = functools.partial(pair_sum_kernel, virt=virt)
    return pl.pallas_call(
        kernel,
        grid=(rows // virt, columns // wide),
        in_specs=[pl.BlockSpec((virt, wide), out_map)],
        out_specs=[pl.BlockSpec((virt, wide), out_map)] * 2,
        out_shape=[
            jax.ShapeDtypeStruct((rows, columns), jnp.bfloat16),
            jax.ShapeDtypeStruct((rows, columns), SMALL),
        ],
        compiler_params=pltpu.CompilerParams(vmem_limit_bytes=VMEM_BYTES),
        cost_estimate=pl.CostEstimate(
            flops=rows * columns * 8,
            bytes_accessed=rows * columns * 5,
            transcendentals=0,
        ),
        name="pair_sum",
    )(integrals)


def product_kernel(where_ref, head_ref, rest_ref, amp_ref, *others):
    out_ref = others[-1]
    amp = amp_ref[...]
    small = (amp.astype(jnp.float32) * AMP_SCALE).astype(SMALL)
    fine = jnp.dot(rest_ref[...], small, preferred_element_type=jnp.float32)
    term = jnp.dot(head_ref[...], amp, preferred_element_type=jnp.float32) + fine * UNSCALE

    @pl.when(pl.program_id(0) == 0)
    def _():
        out_ref[...] = term if len(others) == 1 else others[0][...] + term

    @pl.when(pl.program_id(0) != 0)
    def _():
        out_ref[...] += term


def product(where, head, rest, amp, so_far, rows, depth, parts, part):
    columns = amp.shape[1]
    steps = amp.shape[0] // depth
    left = pl.BlockSpec((rows, depth), lambda k, w: (w[0], k * parts + part))
    in_specs = [left, left, pl.BlockSpec((depth, columns), lambda k, w: (k, 0))]
    args = [head, rest, amp]
    if so_far is not None:
        in_specs.append(pl.BlockSpec((rows, columns), lambda k, w: (w[0], 0)))
        args.append(so_far)
    return pl.pallas_call(
        product_kernel,
        grid_spec=pltpu.PrefetchScalarGridSpec(
            num_scalar_prefetch=1,
            grid=(steps,),
            in_specs=in_specs,
            out_specs=pl.BlockSpec((rows, columns), lambda k, w: (0, 0)),
        ),
        out_shape=jax.ShapeDtypeStruct((rows, columns), jnp.float32),
        compiler_params=pltpu.CompilerParams(vmem_limit_bytes=VMEM_BYTES),
        cost_estimate=pl.CostEstimate(
            flops=3 * rows * columns * amp.shape[0],
            bytes_accessed=rows * amp.shape[0] * 3,
            transcendentals=0,
        ),
        name="product",
    )(where, head, rest, amp, *([] if so_far is None else [so_far]))


def per_device(integrals, amplitudes, source, occ_energy, vir_energy, col_energy):
    virt = vir_energy.shape[0]
    cols = lax.axis_size("col")
    me = lax.axis_index("col")
    rows, depth = integrals.shape
    out_rows, columns = source.shape
    amp_rows = amplitudes.shape[0]
    half = columns // 2
    parts = 2 if amp_rows % (2 * 256) == 0 else 1
    sub = amp_rows // parts

    gather = lambda x: lax.all_gather(x, "row", axis=0, tiled=True)
    amp_first = gather(amplitudes[:, :half])
    amp_later = [gather(amplitudes[p * sub : (p + 1) * sub, half:]) for p in range(parts)]

    head, rest = pair_sum(integrals, virt)

    deep = min(depth, 1024)
    whole = jnp.zeros((1,), jnp.int32)
    first = product(whole, head, rest, amp_first, None, rows, deep, 1, 0)

    def swap(block, step):
        order = [(i, (i + step) % cols) for i in range(cols)]
        return lax.ppermute(block, "col", order)

    def share(total, step):
        return lax.dynamic_slice_in_dim(total, lax.rem(me + step, cols) * out_rows, out_rows, 0)

    got_first = [swap(share(first, s).astype(jnp.float16), s) for s in range(1, cols)]
    kept_first = share(first, 0)

    later = None
    for p in range(parts - 1):
        later = product(whole, head, rest, amp_later[p], later, rows, sub, parts, p)
    last_depth = sub if parts > 1 else deep
    got_later = []
    for s in list(range(1, cols)) + [0]:
        where = lax.rem(me + s, cols).reshape(1)
        block = product(where, head, rest, amp_later[-1], later, out_rows, last_depth, parts, parts - 1)
        if s > 0:
            got_later.append(swap(block.astype(jnp.float16), s))
        else:
            kept_later = block

    def total(kept, got):
        for g in got:
            kept = kept + g.astype(jnp.float32)
        return kept

    summed = jnp.concatenate([total(kept_first, got_first), total(kept_later, got_later)], axis=1)
    start = (lax.axis_index("row") * cols + me) * out_rows
    vir_all = jnp.tile(vir_energy, occ_energy.shape[0])
    occ_all = jnp.repeat(occ_energy, virt)
    vir_part = lax.dynamic_slice_in_dim(vir_all, start, out_rows, 0)
    occ_part = lax.dynamic_slice_in_dim(occ_all, start, out_rows, 0)
    denom = vir_part[:, None] - occ_part[:, None] + col_energy[None, :]
    return -(source + summed) / denom


def solution(mesh):
    in_specs = (P("row", "col"), P(("col", "row"), None), P(("row", "col"), None), P(), P(), P())
    out_specs = P(("row", "col"), None)
    return jax.shard_map(
        per_device, mesh=mesh, in_specs=in_specs, out_specs=out_specs, check_vma=False
    )
```

time: 478 us -> 402 us (0.84)
  Pallas kernels: 0 us -> 232 us
  local copies, waits for them, and re-layouts: 215 us -> 6.25 us
  matrix products: 182 us -> 0 us
  waiting for transfers between devices: 58.8 us -> 136 us
    pallas_call x0 -> x5, Pallas kernels: none -> 232 us  [the longest x4 160 us: product(): pl.pallas_call(product_kernel, grid_spec=pltpu.PrefetchScalarGridSpec(num...]
    dot_general x4 -> x0, matrix products: 182 us -> none  [the longest x2 93 us: both_rows(): jnp.dot(integrals, gathered, preferred_element_type=jnp.float32)]
    dot_general x2 -> x0, local copies, waits for them, and re-layouts: 147 us -> none  [summed_terms(): lax.dot_general(blocks, amp_blocks, (((1, 2), (1, 0)), ((), ())), preferr...]
    all_gather x1 -> x3, waiting for transfers between devices: 0.01 us -> 135 us  [per_device(): gather = lambda x: lax.all_gather(x, 'row', axis=0, tiled=True)]
    reduce_scatter x2 -> x0, waiting for transfers between devices: 58.1 us -> none  [half_sum(): lax.psum_scatter(both_rows(jnp.int32(0), lax.axis_size('col') * out_rows)...]
    unnamed x11 -> x18, local copies, waits for them, and re-layouts: 44.8 us -> 1.71 us
    slice x1 -> x2, local copies, waits for them, and re-layouts: 22.6 us -> 4.54 us  [the longest x1 2.27 us: per_device(): amplitudes[p * sub:(p + 1) * sub, half:]]
  transfers between devices with their start and end apart: 3 -> 5, of which waited for: 1 -> 3; matrix products, arithmetic and copies ran while one was open for 60% -> 2% of each run, Pallas kernels for 0% -> 58%
where the time goes in v1:
time: 402 us; the launch traced here: 400 us
  Pallas kernels  232 us (58%)
  waiting for transfers between devices  136 us (34%)
  between operations  13.2 us (3%)
  other arithmetic  9.61 us (2%)
  local copies, waits for them, and re-layouts  6.25 us (2%)
    pallas_call x4, Pallas kernels, product(): pl.pallas_call(product_kernel, grid_spec=pltpu.PrefetchScalarGridSpec(num...  160 us
    all_gather x3, waiting for transfers between devices, per_device(): gather = lambda x: lax.all_gather(x, 'row', axis=0, tiled=True)  135 us
    pallas_call x1, Pallas kernels, pair_sum(): pl.pallas_call(kernel, grid=(rows // virt, columns // wide), in_specs=[pl...  71.8 us
  transfers between devices with their start and end apart: 5, of which 3 were waited for; matrix products, arithmetic and copies ran while one was open for 2% of the time, Pallas kernels for 58%

profile of v1, /device:TPU:0, one launch (start us, length us, event | category | flops | bytes accessed | tf_op | source)
XLA Modules:
  0.0 400.1 jit_solution(10992700278516995887)
XLA Ops:
  6.5 0.0 copy-start
  6.5 0.0 copy-start.6
  6.5 0.0 all-gather.8.cloned.1.call-start
  6.5 2.3 fusion.2
  8.8 0.0 all-gather.8.cloned.1.call-update
  8.8 0.0 all-gather.6.cloned.1.call-start
  8.9 0.7 all-gather.6.cloned.1.call-update
  9.6 0.0 all-gather.4.cloned.1.call-start
  9.6 2.3 slice.9
  11.9 0.0 all-gather.4.cloned.1.call-update
  12.0 0.0 copy-done
  12.0 0.0 copy-done.6
  12.0 0.1 broadcast_bitcast_fusion
  12.2 71.8 %pair_sum.1 = (bf16[2048,16384]{1,0:T(8,128)(2,1)}, f8e5m2[2048,16384]{1,0:T(32,128)(4,1)}) custom-call(bf16[2048,16384]{1,0:T(8,128)(2,1)} %block_ref.1), custom_call_target="tpu_custom_call" | custom-call | flops 268435456 | bytes 167772160 | tf_op jit(solution)/shard_map/pair_sum/pallas_call | solution.py:33
  84.0 0.6 dynamic-slice_subtract_fusion
  84.6 2.5 all-gather.8.cloned.1.call-done.amp_ref
  87.2 40.6 %product.5.others_0_ = f32[2048,512]{1,0:T(8,128)} custom-call(s32[1]{0:T(128)} %constant.9.clone.1.where_ref, bf16[2048,16384]{1,0:T(8,128)(2,1)} %get-tuple-element.7.head_ref, f8e5m2[2048,16384]{1,0:T(32,128)(4,1)} %get-tuple-element.8.rest_ref, bf16[8192,512]{1,0:T(8,128)(2,1)} %all-gather.8.cloned.1.call-done.amp_ref), custom_call_target="tpu_custom_call" | custom-call | flops 25769803776 | bytes 50331648 | tf_op jit(solution)/shard_map/product/pallas_call | solution.py:77
  127.8 34.7 %all-gather.6.cloned.1.call-done.amp_ref = bf16[8192,512]{1,0:T(8,128)(2,1)} async-done(((bf16[512,512]{1,0:T(8,128)(2,1)}), bf16[8192,512]{1,0:T(8,128)(2,1)}) %all-gather.6.cloned.1.call-update) | async-done | bytes 8388624 | tf_op jit(solution)/shard_map/all_gather | solution.py:107
  162.5 26.2 %product.7 = f32[1024,512]{1,0:T(8,128)} custom-call(s32[1]{0:T(128)} %bitcast.1.where_ref, bf16[2048,16384]{1,0:T(8,128)(2,1)} %get-tuple-element.7.head_ref, f8e5m2[2048,16384]{1,0:T(32,128)(4,1)} %get-tuple-element.8.rest_ref, bf16[8192,512]{1,0:T(8,128)(2,1)} %all-gather.6.cloned.1.call-done.amp_ref, f32[2048,512]{1,0:T(8,128)} %product.5.others_0_), custom_call_target="tpu_custom_call" | custom-call | flops 12884901888 | bytes 25165824 | tf_op jit(solution)/shard_map/product/pallas_call | solution.py:77
  188.7 1.8 convert_element_type.14
  190.5 1.3 collective-permute-start.1
  191.9 98.0 %all-gather.4.cloned.1.call-done.amp_ref = bf16[16384,512]{1,0:T(8,128)(2,1)} async-done(((bf16[1024,512]{1,0:T(8,128)(2,1)}), bf16[16384,512]{1,0:T(8,128)(2,1)}) %all-gather.4.cloned.1.call-update) | async-done | bytes 16777232 | tf_op jit(solution)/shard_map/all_gather | solution.py:107
  289.8 67.8 %product.4 = f32[2048,512]{1,0:T(8,128)} custom-call(s32[1]{0:T(128)} %constant.9.clone.1.where_ref, bf16[2048,16384]{1,0:T(8,128)(2,1)} %get-tuple-element.7.head_ref, f8e5m2[2048,16384]{1,0:T(32,128)(4,1)} %get-tuple-element.8.rest_ref, bf16[16384,512]{1,0:T(8,128)(2,1)} %all-gather.4.cloned.1.call-done.amp_ref), custom_call_target="tpu_custom_call" | custom-call | flops 51539607552 | bytes 100663296 | tf_op jit(solution)/shard_map/product/pallas_call | solution.py:77
  357.6 1.8 dynamic-slice_convert_fusion
  359.5 1.5 collective-permute-start
  361.0 25.7 %product.6 = f32[1024,512]{1,0:T(8,128)} custom-call(s32[1]{0:T(128)} %bitcast.where_ref, bf16[2048,16384]{1,0:T(8,128)(2,1)} %get-tuple-element.7.head_ref, f8e5m2[2048,16384]{1,0:T(32,128)(4,1)} %get-tuple-element.8.rest_ref, bf16[8192,512]{1,0:T(8,128)(2,1)} %all-gather.6.cloned.1.call-done.amp_ref, f32[2048,512]{1,0:T(8,128)} %product.5.others_0_), custom_call_target="tpu_custom_call" | custom-call | flops 12884901888 | bytes 25165824 | tf_op jit(solution)/shard_map/product/pallas_call | solution.py:77
  386.7 0.0 copy-start.2
  386.7 0.0 copy-start.3
  386.7 0.0 copy-start.4
  386.7 0.0 copy-start.5
  386.7 0.0 collective-permute-done.1
  386.7 2.1 convert_add_fusion
  388.9 0.0 collective-permute-done
  388.9 0.6 copy-done.2
  389.5 0.0 copy-start.1
  389.5 0.4 convert_add_fusion.1
  389.9 0.9 copy-done.3
  390.8 0.0 copy-done.4
  390.8 0.0 copy-done.5
  390.8 2.8 fusion.1
  393.6 0.0 copy-done.1
  (3 shorter events, 0.1 us)
Async XLA Ops:
  6.5 5.4 %copy-start = (f32[512]{0:T(512)S(1)}, f32[512]{0:T(512)}, u32[]{:S(2)}) copy-start(f32[512]{0:T(512)} %param.10) | copy-start | bytes 6148
  6.5 5.5 %copy-start.6 = (f32[64]{0:T(128)S(1)}, f32[64]{0:T(128)}, u32[]{:S(2)}) copy-start(f32[64]{0:T(128)} %param.9) | copy-start | bytes 772
  6.5 80.6 %all-gather.8.cloned.1.call-start = ((), (), s32[]{:S(2)}) async-start(), calls=%async_computation.2 | async-start | bytes 8912896 | tf_op jit(solution)/shard_map/all_gather | solution.py:107
  8.8 153.6 %all-gather.6.cloned.1.call-start = ((), (), s32[]{:S(2)}) async-start(), calls=%async_computation.1 | async-start | bytes 8912896 | tf_op jit(solution)/shard_map/all_gather | solution.py:107
  9.6 280.2 %all-gather.4.cloned.1.call-start = ((), (), s32[]{:S(2)}) async-start(), calls=%async_computation | async-start | bytes 17825792 | tf_op jit(solution)/shard_map/all_gather | solution.py:107
  190.5 196.2 %collective-permute-start.1 = (f16[1024,512]{1,0:T(8,128)(2,1)S(1)}, f16[1024,512]{1,0:T(8,128)(2,1)S(1)}, u32[]{:S(2)}, u32[]{:S(2)}) collective-permute-start(f16[1024,512]{1,0:T(8,128)(2,1)S(1)} %convert_element_type.14), channel_id=1, source_target_pairs={{0,1},{1,0},{2,3},{3,2},{4,5},{5,4},{6,7},{7,6},{8,9},{9,8},{10,11... | collective-permute-start | bytes 3145736 | tf_op jit(solution)/shard_map/ppermute | solution.py:119
  359.5 29.4 %collective-permute-start = (f16[1024,512]{1,0:T(8,128)(2,1)S(1)}, f16[1024,512]{1,0:T(8,128)(2,1)S(1)}, u32[]{:S(2)}, u32[]{:S(2)}) collective-permute-start(f16[1024,512]{1,0:T(8,128)(2,1)S(1)} %dynamic-slice_convert_fusion), channel_id=1, source_target_pairs={{0,1},{1,0},{2,3},{3,2},{4,5},{5,4},{6,7},{7,6},{8,9},{9,8},{10,11... | collective-permute-start | bytes 3145736 | tf_op jit(solution)/shard_map/ppermute | solution.py:119
  386.7 2.8 copy-start.2
  386.7 4.1 %copy-start.3 = (f32[1024,1024]{1,0:T(8,128)S(1)}, f32[1024,1024]{1,0:T(8,128)}, u32[]{:S(2)}) copy-start(f32[1024,1024]{1,0:T(8,128)} %param.8) | copy-start | bytes 12582916
  386.7 4.1 %copy-start.4 = (f32[1024]{0:T(1024)S(1)}, f32[1024]{0:T(1024)}, u32[]{:S(2)}) copy-start(f32[1024]{0:T(1024)} %dynamic-slice_subtract_fusion) | copy-start | bytes 12292
  386.7 4.1 %copy-start.5 = (f32[1024]{0:T(1024)S(1)}, f32[1024]{0:T(1024)}, u32[]{:S(2)}) copy-start(f32[1024]{0:T(1024)} %param.11) | copy-start | bytes 12292
  389.5 4.1 %copy-start.1 = (f32[512]{0:T(512)S(1)}, f32[512]{0:T(512)}, u32[]{:S(2)}) copy-start(f32[512]{0:T(512)} %param.10) | copy-start | bytes 6148
Sparse Core Ops, SparseCore 0:
  9.5 77.5 all-gather.7
  89.3 73.1 all-gather.5
  164.7 125.1 all-gather.3
